TPU v7x, 32 devices: a whole 2x2x4 slice. The times are simulated.
32 devices in a mesh: rep: 2 (over x), blk: 8 (over z, y), width: 2 (over core).
Axes of the slice: x: 2, y: 2, z: 4, core: 2. Of those that a mesh axis runs over, the one named last changes fastest.
Arguments:
- tokens: bfloat16 [256, 16384], P(('rep', 'blk'), 'width'), parts along dimension 0, may hold values from -6 to 6
- norm_gain: float32 [16384], P('width'), as said below
- w_query: bfloat16 [16384, 8192], P('width', 'blk'), may hold values from -0.046875 to 0.046875
- w_key: bfloat16 [16384, 512], P('width', 'blk'), may hold values from -0.046875 to 0.046875
- w_value: bfloat16 [16384, 512], P('width', 'blk'), may hold values from -0.046875 to 0.046875
- w_output: bfloat16 [8192, 16384], P('blk', 'width'), may hold values from -0.0625 to 0.0625
- seq_ids: int32 [256], P('rep'), parts along dimension 0, may hold values from 0 to 7, never falling along the last dimension, each value on 1 to 32 neighbouring positions
Outputs:
- attended: bfloat16 [256, 16384], P(('rep', 'blk'), 'width'), parts along dimension 0
There are 2 independent parts, one for each index of `rep`. A program takes and returns all parts, laid end to end along the dimension named above; an argument that names none is the same for every part. Nothing has to cross between parts.
Inputs may be any that keep to these rules, and one draw needn't show every extreme that they name: `norm_gain`: Positive. `seq_ids`: never falling; each of the 8 sequences holds consecutive tokens, 1 to 32 of them, and one holds exactly 32.
All inputs are finite; a program needn't handle non-finite values.
Results may differ from a plain program's by a relative error of at most 0.035.
Values may be sent and summed in bfloat16 or wider, within the bound.
A program may use at most 128 MiB of HBM per device.

v0:
```python
import jax
import jax.numpy as jnp
from jax import lax
from jax.sharding import PartitionSpec as P

HEADS = 64
KV_HEADS = 4
HEAD = 128


EPSILON = 1e-05


def rotate(values_in, positions):
    half_dim = values_in.shape[-1] // 2
    freqs = 500000.0 ** (-2.0 * jnp.arange(half_dim, dtype=jnp.float32) / values_in.shape[-1])
    angles = positions.astype(jnp.float32)[:, None] * freqs[None, :]
    cosine = jnp.cos(angles)[:, None, :]
    sine = jnp.sin(angles)[:, None, :]
    lower = values_in[..., :half_dim]
    upper = values_in[..., half_dim:]
    return jnp.concatenate([lower * cosine - upper * sine, upper * cosine + lower * sine], axis=-1)


def local(tokens, norm_gain, w_query, w_key, w_value, w_output, seq_ids):
    rows_blk, half_width = tokens.shape
    width_full = half_width * lax.axis_size("width")
    total_rows = rows_blk * lax.axis_size("blk")
    floats = tokens.astype(jnp.float32)
    row_squares = lax.psum(jnp.sum(floats * floats, axis=1), "width")
    normed = (
        floats * lax.rsqrt(row_squares / width_full + EPSILON)[:, None] * norm_gain[None, :]
    ).astype(jnp.bfloat16)
    query_cols = w_query.shape[1]
    kv_width = w_key.shape[1]
    weights_all = jnp.concatenate([w_query, w_key, w_value], axis=1)
    partial_sums = jnp.dot(
        lax.all_gather(normed, "blk", axis=0, tiled=True),
        weights_all,
        preferred_element_type=jnp.float32,
    )
    summed = lax.psum(partial_sums, "width")
    q_raw = summed[:, :query_cols]
    kv_raw = summed[:, query_cols:]
    query_rows = q_raw.shape[0]
    stacked = jnp.stack([kv_raw[:, :kv_width], kv_raw[:, kv_width:]])
    every_kv = lax.all_gather(stacked.astype(jnp.bfloat16), "blk", axis=2, tiled=True).astype(
        stacked.dtype
    )
    heads_dev = query_cols // HEAD
    group = HEADS // KV_HEADS
    kv_index = lax.axis_index("blk") * heads_dev // group
    split_heads = every_kv.reshape(2, total_rows, HEAD, KV_HEADS)
    own_head = lax.dynamic_index_in_dim(split_heads, kv_index, 3, keepdims=False)
    keys_raw = own_head[0]
    values_raw = own_head[1]
    index_row = jnp.arange(total_rows, dtype=jnp.int32)
    starts = jnp.sum((seq_ids[None, :] < seq_ids[:, None]).astype(jnp.int32), axis=1)
    positions = index_row - starts
    queries = rotate(q_raw.reshape(query_rows, heads_dev, HEAD), positions).astype(jnp.bfloat16)
    keys_rot = rotate(keys_raw[:, None, :], positions)[:, 0, :].astype(jnp.bfloat16)
    values_bf = values_raw.astype(jnp.bfloat16)
    scores = jnp.einsum(
        "thd,sd->hts", queries, keys_rot, preferred_element_type=jnp.float32
    ) / jnp.sqrt(jnp.float32(HEAD))
    allowed = (seq_ids[None, :] == seq_ids[:, None]) & (index_row[None, :] <= index_row[:, None])
    scores = jnp.where(allowed[None], scores, jnp.float32(-jnp.inf))
    row_top = jnp.max(scores, axis=-1, keepdims=True)
    raised = jnp.exp(scores - row_top)
    probs = (raised / jnp.sum(raised, axis=-1, keepdims=True)).astype(jnp.bfloat16)
    context = jnp.einsum("hts,sd->thd", probs, values_bf, preferred_element_type=jnp.float32)
    context = context.astype(jnp.bfloat16).reshape(query_rows, query_cols)
    complete = lax.psum(
        jnp.dot(context, w_output, preferred_element_type=jnp.float32).astype(jnp.bfloat16), "blk"
    ).astype(jnp.float32)
    result = lax.dynamic_slice_in_dim(complete, lax.axis_index("blk") * rows_blk, rows_blk, 0)
    return result.astype(jnp.bfloat16)


def solution(mesh):
    placed = (
        P(("rep", "blk"), "width"),
        P("width"),
        P("width", "blk"),
        P("width", "blk"),
        P("width", "blk"),
        P("blk", "width"),
        P("rep"),
    )
    return jax.shard_map(
        local, mesh=mesh, in_specs=placed, out_specs=P(("rep", "blk"), "width"), check_vma=False
    )
```

profile of v0, /device:TPU:0, one launch (start us, length us, event | category | flops | bytes accessed | tf_op | source)
XLA Modules:
  0.0 248.4 jit_solution(16197910274421131205)
XLA Ops:
  6.5 1.2 fusion.5
  7.8 2.6 %psum.21 = f32[16]{0:T(128)S(1)} all-reduce(f32[16]{0:T(128)S(1)} %fusion.5), channel_id=1, replica_groups=mesh['rep'=2,'blk'=8,'width'=2] {'width'}, use_global_device_ids=true, to_apply=%region_1.0 | all-reduce | flops 16 | bytes 128 | tf_op jit(solution)/shard_map/psum | solution.py:30
  10.3 1.8 fusion.7
  12.2 2.0 copy.32
  14.3 1.8 copy.33
  16.1 27.6 %concatenate.11 = bf16[8192,1152]{1,0:T(8,128)(2,1)} concatenate(bf16[8192,1024]{1,0:T(8,128)(2,1)} %param.9, bf16[8192,64]{1,0:T(8,128)(2,1)S(1)} %copy.32, bf16[8192,64]{1,0:T(8,128)(2,1)} %copy.33), dimensions={1} | concatenate | bytes 37748736 | tf_op jit(solution)/shard_map/concatenate | solution.py:36
  43.7 20.4 %all-gather.2.cloned.1.call-done = bf16[128,8192]{1,0:T(8,128)(2,1)} async-done(((bf16[16,8192]{1,0:T(8,128)(2,1)}), bf16[128,8192]{1,0:T(8,128)(2,1)}) %all-gather.2.cloned.1.call-update) | async-done | bytes 2097168 | tf_op jit(solution)/shard_map/all_gather | solution.py:38
  64.2 10.7 %fusion.34 = f32[128,1152]{1,0:T(8,128)} fusion(bf16[128,8192]{1,0:T(8,128)(2,1)} %all-gather.2.cloned.1.call-done, bf16[8192,1152]{1,0:T(8,128)(2,1)} %concatenate.11), kind=kOutput, calls=%fused_computation.54 | convolution fusion | flops 2415919104 | bytes 21561344 | tf_op jit(solution)/shard_map/dot_general | solution.py:37
  75.1 0.3 multiply_cosine_fusion
  75.4 17.0 %all-reduce.3.cloned.1.call-done = f32[128,1152]{1,0:T(8,128)} async-done(((f32[128,1152]{1,0:T(8,128)}), f32[128,1152]{1,0:T(8,128)}) %all-reduce.3.cloned.1.call-update) | async-done | bytes 589840 | tf_op jit(solution)/shard_map/psum | solution.py:42
  92.4 1.1 convert.24
  93.6 0.1 copy.34
  93.7 31.1 %all_gather.7 = bf16[2,128,512]{1,0,2:T(2,128)(2,1)S(1)} all-gather(bf16[2,128,64]{1,0,2:T(2,128)(2,1)S(1)} %copy.34), channel_id=1, replica_groups=mesh['rep'=2,'blk'=8,'width'=2] {'blk'}, dimensions={2}, use_global_device_ids=true | all-gather | bytes 294912 | tf_op jit(solution)/shard_map/all_gather | solution.py:47
  124.9 0.1 dynamic-slice_convert_fusion
  125.0 0.2 fusion.19
  125.2 1.1 slice_bitcast_fusion
  126.4 0.2 fusion.30
  126.6 0.2 subtract_convert_fusion
  126.8 0.3 fusion.4
  127.1 0.4 fusion.31
  127.6 0.3 convolution_convert_fusion.1
  127.9 9.5 %convolution_convert_fusion = bf16[128,8192]{1,0:T(8,128)(2,1)} fusion(bf16[128,1024]{0,1:T(8,128)(2,1)S(1)} %bitcast.46, bf16[1024,8192]{1,0:T(8,128)(2,1)} %param.12), kind=kOutput, calls=%fused_computation.1 | convolution fusion | flops 2148532224 | bytes 19136512 | tf_op jit(solution)/shard_map/dot_general | solution.py:74
  137.4 102.7 %all-reduce.5.cloned.1.call-done = bf16[128,8192]{1,0:T(8,128)(2,1)} async-done(((bf16[128,8192]{1,0:T(8,128)(2,1)}), bf16[128,8192]{1,0:T(8,128)(2,1)}) %all-reduce.5.cloned.1.call-update) | async-done | bytes 2097168 | tf_op jit(solution)/shard_map/psum | solution.py:73
  240.2 1.7 convert_convert_fusion
  (20 shorter events, 0.6 us)
Async XLA Ops:
  6.5 7.7 %copy-start = (bf16[8192,64]{0,1:T(8,128)(2,1)S(1)}, bf16[8192,64]{0,1:T(8,128)(2,1)}, u32[]{:S(2)}) copy-start(bf16[8192,64]{0,1:T(8,128)(2,1)} %param.11) | copy-start | bytes 3145732
  6.5 57.6 %all-gather.2.cloned.1.call-start = ((), (), s32[]{:S(2)}) async-start(), calls=%async_computation | async-start | bytes 2359296 | tf_op jit(solution)/shard_map/all_gather | solution.py:38
  12.2 80.2 %all-reduce.3.cloned.1.call-start = ((), (), s32[]{:S(2)}) async-start(), calls=%async_computation.1 | async-start | bytes 1179648 | tf_op jit(solution)/shard_map/psum | solution.py:42
  16.1 27.6 %copy-start.1 = (s32[128]{0:T(128)S(1)}, s32[128]{0:T(128)}, u32[]{:S(2)}) copy-start(s32[128]{0:T(128)} %param.13) | copy-start | bytes 1540
  74.9 165.3 %all-reduce.5.cloned.1.call-start = ((), (), s32[]{:S(2)}) async-start(), calls=%async_computation.2 | async-start | bytes 4194304 | tf_op jit(solution)/shard_map/psum | solution.py:73
Sparse Core Ops, SparseCore 0:
  12.3 51.8 all-gather.1
  75.0 17.3 all-reduce.2
  137.5 102.5 all-reduce.4
where the time goes:
time: 249 us; the launch traced here: 248 us
  waiting for transfers between devices  140 us (56%)
  blocking collectives  33.7 us (14%)
  local copies, waits for them, and re-layouts  33 us (13%)
  matrix products  21.3 us (9%)
  between operations  13.3 us (5%)
  other arithmetic  6.83 us (3%)
    psum x1, waiting for transfers between devices, local(): lax.psum(jnp.dot(context, w_output, preferred_element_type=jnp.float32).a...  103 us
    all_gather x1, blocking collectives, local(): lax.all_gather(stacked.astype(jnp.bfloat16), 'blk', axis=2, tiled=True)  31.1 us
    concatenate x1, local copies, waits for them, and re-layouts, local(): weights_all = jnp.concatenate([w_query, w_key, w_value], axis=1)  27.6 us
    all_gather x1, waiting for transfers between devices, local(): lax.all_gather(normed, 'blk', axis=0, tiled=True)  20.4 us
    psum x1, waiting for transfers between devices, local(): summed = lax.psum(partial_sums, 'width')  17 us
    dot_general x1, matrix products, local(): jnp.dot(lax.all_gather(normed, 'blk', axis=0, tiled=True), weights_all, p...  10.7 us
    dot_general x1, matrix products, local(): jnp.dot(context, w_output, preferred_element_type=jnp.float32)  9.53 us
    unnamed x8, local copies, waits for them, and re-layouts  5.02 us
  transfers between devices with their start and end apart: 3, of which 3 were waited for; matrix products, arithmetic and copies ran while one was open for 13% of the time, Pallas kernels for 0%

commit v1 on v0

--- a/solution.py
+++ b/solution.py
@@ -1,19 +1,32 @@
+import functools
+import math
+
 import jax
 import jax.numpy as jnp
 from jax import lax
+from jax.experimental import pallas as pl
+from jax.experimental.pallas import tpu as pltpu
 from jax.sharding import PartitionSpec as P
 
 HEADS = 64
 KV_HEADS = 4
 HEAD = 128
 
-
 EPSILON = 1e-05
+THETA = 500000.0
+
+NZ = 4
+NY = 2
+WIDTH = 2
+CHUNKS = 4
+TILE = 512
+
+NT = (((1,), (1,)), ((), ()))
 
 
 def rotate(values_in, positions):
     half_dim = values_in.shape[-1] // 2
-    freqs = 500000.0 ** (-2.0 * jnp.arange(half_dim, dtype=jnp.float32) / values_in.shape[-1])
+    freqs = THETA ** (-2.0 * jnp.arange(half_dim, dtype=jnp.float32) / values_in.shape[-1])
     angles = positions.astype(jnp.float32)[:, None] * freqs[None, :]
     cosine = jnp.cos(angles)[:, None, :]
     sine = jnp.sin(angles)[:, None, :]
@@ -22,7 +35,7 @@
     return jnp.concatenate([lower * cosine - upper * sine, upper * cosine + lower * sine], axis=-1)
 
 
-def local(tokens, norm_gain, w_query, w_key, w_value, w_output, seq_ids):
+def collective_form(tokens, norm_gain, w_query, w_key, w_value, w_output, seq_ids):
     rows_blk, half_width = tokens.shape
     width_full = half_width * lax.axis_size("width")
     total_rows = rows_blk * lax.axis_size("blk")
@@ -77,6 +90,330 @@
     return result.astype(jnp.bfloat16)
 
 
+def fused_kernel(
+    tok, gain, wq_hbm, wk_hbm, wv_hbm, wo_hbm, seq, out,
+    wq, wk, wv, wo, xg, acc_q, acc_kv, acc_ss, q_send, q_recv, ss_send, ss_recv,
+    kv_send, kv_recv, cos_q, sin_q, cos_k, sin_k, bias, ctx, part, y_part, summed, z_part,
+    w_sem, wo_sem, kvw_sem, gz_send, gz_recv, gy_send, gy_recv,
+    ex_send, ex_recv, kv_ssem, kv_rsem, ry_send, ry_recv, rz_send, rz_recv,
+):
+    rows, width = tok.shape
+    n = NZ * NY
+    total = rows * n
+    cols = wq.shape[1]
+    heads_dev = cols // HEAD
+    kvw = wk.shape[1]
+    per_head = kvw // KV_HEADS
+    span = width // CHUNKS
+    tile = min(TILE, span)
+    half = HEAD // 2
+    f32, bf16 = jnp.float32, jnp.bfloat16
+
+    me = lax.axis_index("blk")
+    core = lax.axis_index("width")
+    y = me % NY
+    z = me // NY
+    other = 1 - core
+    y_peer = z * NY + (1 - y)
+
+    def chunk(c):
+        return pl.ds(c * span, span)
+
+    def z_blk(step):
+        return ((z + step) % NZ) * NY + y
+
+    wq_copies = [
+        pltpu.make_async_copy(wq_hbm.at[chunk(c), :], wq.at[chunk(c), :], w_sem.at[c])
+        for c in range(CHUNKS)
+    ]
+    wo_copies = [
+        pltpu.make_async_copy(wo_hbm.at[:, chunk(c)], wo.at[:, chunk(c)], wo_sem.at[c])
+        for c in range(CHUNKS)
+    ]
+    wk_copy = pltpu.make_async_copy(wk_hbm, wk, kvw_sem.at[0])
+    wv_copy = pltpu.make_async_copy(wv_hbm, wv, kvw_sem.at[1])
+    wk_copy.start()
+    wv_copy.start()
+    for copy in wq_copies + wo_copies:
+        copy.start()
+
+    barrier = pltpu.get_barrier_semaphore()
+    for step in range(n):
+        for side in range(WIDTH):
+            if step == 0 and side == 0:
+                continue
+            pl.semaphore_signal(
+                barrier, inc=1,
+                device_id={"blk": (me + step) % n, "width": (core + side) % WIDTH},
+                device_id_type=pl.DeviceIdType.MESH,
+            )
+    pl.semaphore_wait(barrier, n * WIDTH - 1)
+
+    def remote(src, dst, s_sem, r_sem, blk, side):
+        return pltpu.make_async_remote_copy(
+            src_ref=src, dst_ref=dst, send_sem=s_sem, recv_sem=r_sem,
+            device_id={"blk": blk, "width": side}, device_id_type=pl.DeviceIdType.MESH,
+        )
+
+    def gz(c, d, blk):
+        return remote(tok.at[:, chunk(c)], xg.at[c, blk], gz_send.at[c, d - 1], gz_recv.at[c, d - 1], z_blk(d), core)
+
+    def gy(c, d):
+        src = tok.at[:, chunk(c)] if d == 0 else xg.at[c, z_blk(NZ - d)]
+        return remote(src, xg.at[c, z_blk(NZ - d)], gy_send.at[c, d], gy_recv.at[c, d], y_peer, core)
+
+    def gy_in(c, d):
+        blk = ((z + NZ - d) % NZ) * NY + (1 - y)
+        return remote(tok.at[:, chunk(c)], xg.at[c, blk], gy_send.at[c, d], gy_recv.at[c, d], y_peer, core)
+
+    for c in range(CHUNKS):
+        for d in range(1, NZ):
+            gz(c, d, me).start()
+        gy(c, 0).start()
+
+    for c in range(CHUNKS):
+        xg[c, me] = tok[:, c * span:(c + 1) * span]
+    acc_q[...] = jnp.zeros_like(acc_q)
+    acc_kv[...] = jnp.zeros_like(acc_kv)
+    acc_ss[...] = jnp.zeros_like(acc_ss)
+    by_col = jnp.broadcast_to(seq[...].astype(f32), (total, total))
+    by_row = by_col.T
+    at_row = lax.broadcasted_iota(jnp.int32, (total, total), 0)
+    at_col = lax.broadcasted_iota(jnp.int32, (total, total), 1)
+    starts_q = jnp.sum((by_col < by_row).astype(f32), axis=1, keepdims=True)
+    starts_k = jnp.sum((by_row < by_col).astype(f32), axis=0, keepdims=True)
+    bias[...] = jnp.where((by_col == by_row) & (at_col <= at_row), 0.0, -jnp.inf).astype(f32)
+    rate = -2.0 * math.log(THETA) / HEAD
+    lane = lax.broadcasted_iota(jnp.int32, (total, HEAD), 1)
+    line = lax.broadcasted_iota(jnp.int32, (total, HEAD), 0)
+    angle_q = (line.astype(f32) - starts_q) * jnp.exp((lane % half).astype(f32) * rate)
+    cos_q[...] = jnp.cos(angle_q)
+    sine = jnp.sin(angle_q)
+    sin_q[...] = jnp.where(lane < half, -sine, sine)
+    pos_k = lax.broadcasted_iota(jnp.int32, (half, total), 1).astype(f32) - starts_k
+    angle_k = pos_k * jnp.exp(lax.broadcasted_iota(jnp.int32, (half, total), 0).astype(f32) * rate)
+    cos_k[...] = jnp.cos(angle_k)
+    sin_k[...] = jnp.sin(angle_k)
+
+    def pass_on(c):
+        for d in range(1, NZ):
+            gz(c, d, z_blk(NZ - d)).wait_recv()
+            gy(c, d).start()
+
+    def project(c):
+        def body(k, _):
+            here = pl.ds(pl.multiple_of(k * tile, tile), tile)
+            deep = pl.ds(pl.multiple_of(c * span + k * tile, tile), tile)
+            x = xg[c, :, :, here].reshape(total, tile).astype(f32)
+            squares = x * x
+            folded = squares[:, :HEAD]
+            for i in range(1, tile // HEAD):
+                folded = folded + squares[:, i * HEAD:(i + 1) * HEAD]
+            acc_ss[...] += folded
+            scaled = (x * gain[:, deep]).astype(bf16)
+            acc_q[...] += jnp.dot(scaled, wq[deep, :], preferred_element_type=f32)
+            both = jnp.concatenate([wk[deep, :], wv[deep, :]], axis=1)
+            acc_kv[...] += jnp.dot(scaled, both, preferred_element_type=f32)
+            return 0
+
+        lax.fori_loop(0, span // tile, body, 0)
+
+    pass_on(0)
+    for c in range(CHUNKS):
+        if c + 1 < CHUNKS:
+            pass_on(c + 1)
+        for d in range(NZ):
+            gy_in(c, d).wait_recv()
+        if c == 0:
+            wk_copy.wait()
+            wv_copy.wait()
+        wq_copies[c].wait()
+        project(c)
+
+    rr = lax.broadcasted_iota(jnp.int32, (2 * kvw, 2 * kvw), 0)
+    cc = lax.broadcasted_iota(jnp.int32, (2 * kvw, 2 * kvw), 1)
+    at = ((rr // per_head) % 2) * kvw + (rr % per_head) * KV_HEADS + rr // (2 * per_head)
+    picks = jnp.where(cc == at, 1.0, 0.0).astype(bf16)
+    turned = lax.dot_general(picks, acc_kv[...].astype(bf16), NT, preferred_element_type=f32)
+    kv_send[...] = turned.astype(bf16).reshape(KV_HEADS, 2 * per_head, total)
+    group = HEADS // KV_HEADS
+
+    def kv_copy(step, side, blk, whose):
+        to = (me + step) % n
+        i = step * WIDTH + side
+        return remote(
+            kv_send.at[to * heads_dev // group], kv_recv.at[whose, blk],
+            kv_ssem.at[i], kv_rsem.at[i], to, (core + side) % WIDTH,
+        )
+
+    pairs = [(s, side) for s in range(n) for side in range(WIDTH) if s or side]
+    for s, side in pairs:
+        kv_copy(s, side, me, core).start()
+    kv_recv[core, me] = kv_send[me * heads_dev // group]
+    ss_send[...] = jnp.broadcast_to(jnp.sum(acc_ss[...], axis=1, keepdims=True), (total, HEAD))
+    ss_copy = remote(ss_send, ss_recv, ex_send.at[0], ex_recv.at[0], me, other)
+    ss_copy.start()
+    q_send[...] = acc_q[...].astype(bf16)
+    q_copy = remote(q_send, q_recv, ex_send.at[1], ex_recv.at[1], me, other)
+    q_copy.start()
+
+    ss_copy.wait_recv()
+    scale = lax.rsqrt((ss_send[...] + ss_recv[...]) / (WIDTH * width) + EPSILON)
+    scale_k = scale.T
+    q_copy.wait_recv()
+    for s, side in pairs:
+        kv_copy(s, side, (me + n - s) % n, (core + side) % WIDTH).wait_recv()
+    kv = kv_recv[0].astype(f32) + kv_recv[1].astype(f32)
+    keys = kv[:, :per_head].reshape(HEAD, total) * scale_k
+    values = (kv[:, per_head:].reshape(HEAD, total) * scale_k).astype(bf16)
+    low, high = keys[:half], keys[half:]
+    keys = jnp.concatenate(
+        [low * cos_k[...] - high * sin_k[...], high * cos_k[...] + low * sin_k[...]], axis=0
+    ).astype(bf16)
+    for h in range(heads_dev):
+        own = slice(h * HEAD, (h + 1) * HEAD)
+        q = (acc_q[:, own] + q_recv[:, own].astype(f32)) * scale
+        q = (q * cos_q[...] + pltpu.roll(q, half, 1) * sin_q[...]).astype(bf16)
+        scores = jnp.dot(q, keys, preferred_element_type=f32) * (1.0 / math.sqrt(HEAD)) + bias[...]
+        raised = jnp.exp(scores - jnp.max(scores, axis=1, keepdims=True))
+        probs = (raised / jnp.sum(raised, axis=1, keepdims=True)).astype(bf16)
+        ctx[:, own] = lax.dot_general(probs, values, NT, preferred_element_type=f32).astype(bf16)
+
+    def ry(c):
+        return remote(part.at[c, 1 - y], y_part.at[c], ry_send.at[c], ry_recv.at[c], y_peer, core)
+
+    def rz(c, d):
+        return remote(
+            summed.at[c, (z + d) % NZ], z_part.at[c, d - 1],
+            rz_send.at[c, d - 1], rz_recv.at[c, d - 1], z_blk(d), core,
+        )
+
+    def multiply(c):
+        wo_copies[c].wait()
+
+        def body(k, _):
+            here = pl.ds(pl.multiple_of(k * tile, tile), tile)
+            deep = pl.ds(pl.multiple_of(c * span + k * tile, tile), tile)
+            got = jnp.dot(ctx[...], wo[:, deep], preferred_element_type=f32).astype(bf16)
+            got = got.reshape(NZ, NY, rows, tile)
+            for i in range(NY):
+                part[c, i, :, :, here] = got[:, i]
+            return 0
+
+        lax.fori_loop(0, span // tile, body, 0)
+        ry(c).start()
+
+    def add_y(c):
+        ry(c).wait_recv()
+
+        def body(k, _):
+            here = pl.ds(pl.multiple_of(k * tile, tile), tile)
+            summed[c, :, :, here] = (
+                part[c, y, :, :, here].astype(f32) + y_part[c, :, :, here].astype(f32)
+            ).astype(bf16)
+            return 0
+
+        lax.fori_loop(0, span // tile, body, 0)
+        for d in range(1, NZ):
+            rz(c, d).start()
+
+    def add_z(c):
+        for d in range(1, NZ):
+            rz(c, d).wait_recv()
+        found = summed[c, z].astype(f32)
+        for d in range(1, NZ):
+            found = found + z_part[c, d - 1].astype(f32)
+        out[:, c * span:(c + 1) * span] = found.astype(bf16)
+
+    for c in range(CHUNKS):
+        multiply(c)
+        if c > 0:
+            add_y(c - 1)
+    add_y(CHUNKS - 1)
+    for c in range(CHUNKS):
+        add_z(c)
+
+    for c in range(CHUNKS):
+        for d in range(1, NZ):
+            gz(c, d, me).wait_send()
+            rz(c, d).wait_send()
+        for d in range(NZ):
+            gy(c, d).wait_send()
+        ry(c).wait_send()
+    for s, side in pairs:
+        kv_copy(s, side, me, core).wait_send()
+    ss_copy.wait_send()
+    q_copy.wait_send()
+
+
+def kernel_form(tokens, norm_gain, w_query, w_key, w_value, w_output, seq_ids):
+    rows, width = tokens.shape
+    n = NZ * NY
+    total = rows * n
+    cols = w_query.shape[1]
+    kvw = w_key.shape[1]
+    per_head = kvw // KV_HEADS
+    span = width // CHUNKS
+    bf16, f32 = jnp.bfloat16, jnp.float32
+    vmem = pl.BlockSpec(memory_space=pltpu.VMEM)
+    hbm = pl.BlockSpec(memory_space=pl.ANY)
+    dma = pltpu.SemaphoreType.DMA
+    return pl.pallas_call(
+        fused_kernel,
+        out_shape=jax.ShapeDtypeStruct((rows, width), bf16),
+        in_specs=[vmem, vmem, hbm, hbm, hbm, hbm, vmem],
+        out_specs=vmem,
+        scratch_shapes=[
+            pltpu.VMEM((width, cols), bf16),
+            pltpu.VMEM((width, kvw), bf16),
+            pltpu.VMEM((width, kvw), bf16),
+            pltpu.VMEM((cols, width), bf16),
+            pltpu.VMEM((CHUNKS, n, rows, span), bf16),
+            pltpu.VMEM((total, cols), f32),
+            pltpu.VMEM((total, 2 * kvw), f32),
+            pltpu.VMEM((total, HEAD), f32),
+            pltpu.VMEM((total, cols), bf16),
+            pltpu.VMEM((total, cols), bf16),
+            pltpu.VMEM((total, HEAD), f32),
+            pltpu.VMEM((total, HEAD), f32),
+            pltpu.VMEM((KV_HEADS, 2 * per_head, total), bf16),
+            pltpu.VMEM((WIDTH, n, 2 * per_head, total), bf16),
+            pltpu.VMEM((total, HEAD), f32),
+            pltpu.VMEM((total, HEAD), f32),
+            pltpu.VMEM((HEAD // 2, total), f32),
+            pltpu.VMEM((HEAD // 2, total), f32),
+            pltpu.VMEM((total, total), f32),
+            pltpu.VMEM((total, cols), bf16),
+            pltpu.VMEM((CHUNKS, NY, NZ, rows, span), bf16),
+            pltpu.VMEM((CHUNKS, NZ, rows, span), bf16),
+            pltpu.VMEM((CHUNKS, NZ, rows, span), bf16),
+            pltpu.VMEM((CHUNKS, NZ - 1, rows, span), bf16),
+            dma((CHUNKS,)),
+            dma((CHUNKS,)),
+            dma((2,)),
+            dma((CHUNKS, NZ - 1)),
+            dma((CHUNKS, NZ - 1)),
+            dma((CHUNKS, NZ)),
+            dma((CHUNKS, NZ)),
+            dma((2,)),
+            dma((2,)),
+            dma((n * WIDTH,)),
+            dma((n * WIDTH,)),
+            dma((CHUNKS,)),
+            dma((CHUNKS,)),
+            dma((CHUNKS, NZ - 1)),
+            dma((CHUNKS, NZ - 1)),
+        ],
+        compiler_params=pltpu.CompilerParams(
+            collective_id=0, has_side_effects=True, vmem_limit_bytes=60 * 1024 * 1024
+        ),
+        name="attention_block",
+    )(
+        tokens, norm_gain.reshape(1, width), w_query, w_key, w_value, w_output,
+        seq_ids.reshape(1, total),
+    )
+
+
 def solution(mesh):
     placed = (
         P(("rep", "blk"), "width"),
@@ -87,6 +424,8 @@
         P("blk", "width"),
         P("rep"),
     )
+    on_grid = mesh.shape["blk"] == NZ * NY and mesh.shape["width"] == WIDTH
     return jax.shard_map(
-        local, mesh=mesh, in_specs=placed, out_specs=P(("rep", "blk"), "width"), check_vma=False
+        kernel_form if on_grid else collective_form,
+        mesh=mesh, in_specs=placed, out_specs=P(("rep", "blk"), "width"), check_vma=False,
     )

time: 249 us -> 86.3 us (0.35)
  waiting for transfers between devices: 140 us -> 0 us
  Pallas kernels: 0 us -> 78.9 us
  blocking collectives: 33.7 us -> 0 us
  local copies, waits for them, and re-layouts: 33 us -> 7.17 us
  matrix products: 21.3 us -> 0 us
  between operations: 13.3 us -> 0.01 us
  other arithmetic: 6.83 us -> 0 us
    psum x2 -> x0, waiting for transfers between devices: 120 us -> none  [the longest x1 103 us: local(): lax.psum(jnp.dot(context, w_output, preferred_element_type=jnp.float32).a...]
    pallas_call x0 -> x1, Pallas kernels: none -> 78.9 us  [kernel_form(): pl.pallas_call(fused_kernel, out_shape=jax.ShapeDtypeStruct((rows, width)...]
    all_gather x1 -> x0, blocking collectives: 31.1 us -> none  [local(): lax.all_gather(stacked.astype(jnp.bfloat16), 'blk', axis=2, tiled=True)]
    concatenate x1 -> x0, local copies, waits for them, and re-layouts: 27.6 us -> none  [local(): weights_all = jnp.concatenate([w_query, w_key, w_value], axis=1)]
    dot_general x4 -> x0, matrix products: 20.9 us -> none  [the longest x1 10.7 us: local(): jnp.dot(lax.all_gather(normed, 'blk', axis=0, tiled=True), weights_all, p...]
    all_gather x1 -> x0, waiting for transfers between devices: 20.4 us -> none  [local(): lax.all_gather(normed, 'blk', axis=0, tiled=True)]
    convert_element_type x3 -> x0, other arithmetic: 3.46 us -> none  [the longest x1 1.79 us: local(): normed = (floats * lax.rsqrt(row_squares / width_full + EPSILON)[:, None]...]
    psum x1 -> x0, blocking collectives: 2.58 us -> none  [local(): row_squares = lax.psum(jnp.sum(floats * floats, axis=1), 'width')]
  transfers between devices with their start and end apart: 3 -> 0, of which waited for: 3 -> 0; matrix products, arithmetic and copies ran while one was open for 13% -> 0% of each run, Pallas kernels for 0% -> 0%
where the time goes in v1:
time: 86.3 us; the launch traced here: 86.1 us
  Pallas kernels  78.9 us (91%)
  local copies, waits for them, and re-layouts  7.17 us (8%)
    pallas_call x1, Pallas kernels, kernel_form(): pl.pallas_call(fused_kernel, out_shape=jax.ShapeDtypeStruct((rows, width)...  78.9 us
    unnamed x3, local copies, waits for them, and re-layouts  7.17 us

profile of v1, /device:TPU:0, one launch (start us, length us, event | category | flops | bytes accessed | tf_op | source)
XLA Modules:
  0.0 86.1 jit_solution(2731184722010820041)
XLA Ops:
  0.0 2.8 %copy.8.wk_hbm = bf16[8192,64]{1,0:T(8,128)(2,1)} copy(bf16[8192,64]{0,1:T(8,128)(2,1)} %param.10) | data formatting | bytes 2097152 | tf_op args[3]
  2.8 2.7 %copy.9.wv_hbm = bf16[8192,64]{1,0:T(8,128)(2,1)} copy(bf16[8192,64]{0,1:T(8,128)(2,1)} %param.11) | data formatting | bytes 2097152 | tf_op args[4]
  5.5 78.9 %attention_block.1 = bf16[16,8192]{1,0:T(8,128)(2,1)} custom-call(bf16[16,8192]{1,0:T(8,128)(2,1)} %tok.1, f32[1,8192]{1,0:T(1,128)} %bitcast.2, bf16[8192,1024]{1,0:T(8,128)(2,1)} %wq_hbm.1, bf16[8192,64]{1,0:T(8,128)(2,1)} %copy.8.wk_hbm, bf16[8192,64]{1,0:T(8,128)(2,1)} %copy.9.wv_hbm, bf16[1024,8192]{1,0:T(8,128)(2,1)} %wo_hbm.1, s32[1,128]{1,0:T(1,128)} %bitcast.3), custom_call_target="tpu_custom_call" | custom-call | tf_op jit(solution)/shard_map/attention_block/pallas_call | solution.py:361
  84.4 1.7 %copy.11 = bf16[16,8192]{1,0:T(8,128)(2,1)} copy(bf16[16,8192]{1,0:T(8,128)(2,1)} %attention_block.1) | data formatting | bytes 524288

commit v2 on v1

--- a/solution.py
+++ b/solution.py
@@ -19,7 +19,7 @@
 NY = 2
 WIDTH = 2
 CHUNKS = 4
-TILE = 512
+TILE = 1024
 
 NT = (((1,), (1,)), ((), ()))
 
@@ -92,7 +92,7 @@
 
 def fused_kernel(
     tok, gain, wq_hbm, wk_hbm, wv_hbm, wo_hbm, seq, out,
-    wq, wk, wv, wo, xg, acc_q, acc_kv, acc_ss, q_send, q_recv, ss_send, ss_recv,
+    wq, wkv, wo, xg, acc_q, acc_kv, acc_ss, q_send, q_recv, ss_send, ss_recv,
     kv_send, kv_recv, cos_q, sin_q, cos_k, sin_k, bias, ctx, part, y_part, summed, z_part,
     w_sem, wo_sem, kvw_sem, gz_send, gz_recv, gy_send, gy_recv,
     ex_send, ex_recv, kv_ssem, kv_rsem, ry_send, ry_recv, rz_send, rz_recv,
@@ -102,7 +102,7 @@
     total = rows * n
     cols = wq.shape[1]
     heads_dev = cols // HEAD
-    kvw = wk.shape[1]
+    kvw = wk_hbm.shape[0]
     per_head = kvw // KV_HEADS
     span = width // CHUNKS
     tile = min(TILE, span)
@@ -119,8 +119,14 @@
     def chunk(c):
         return pl.ds(c * span, span)
 
-    def z_blk(step):
-        return ((z + step) % NZ) * NY + y
+    near = z // 2
+    inner = (1 - near) * z + near * (NZ - 1 - z)
+    inward = (z + 1 - 2 * near) * NY + y
+    outward = (z - 1 + 2 * near) * NY + y
+
+    def place(k):
+        at = (inner, 1 - inner, 2, 3)[k]
+        return (1 - near) * at + near * (NZ - 1 - at)
 
     wq_copies = [
         pltpu.make_async_copy(wq_hbm.at[chunk(c), :], wq.at[chunk(c), :], w_sem.at[c])
@@ -130,8 +136,8 @@
         pltpu.make_async_copy(wo_hbm.at[:, chunk(c)], wo.at[:, chunk(c)], wo_sem.at[c])
         for c in range(CHUNKS)
     ]
-    wk_copy = pltpu.make_async_copy(wk_hbm, wk, kvw_sem.at[0])
-    wv_copy = pltpu.make_async_copy(wv_hbm, wv, kvw_sem.at[1])
+    wk_copy = pltpu.make_async_copy(wk_hbm, wkv.at[0:kvw, :], kvw_sem.at[0])
+    wv_copy = pltpu.make_async_copy(wv_hbm, wkv.at[kvw:2 * kvw, :], kvw_sem.at[1])
     wk_copy.start()
     wv_copy.start()
     for copy in wq_copies + wo_copies:
@@ -155,21 +161,42 @@
             device_id={"blk": blk, "width": side}, device_id_type=pl.DeviceIdType.MESH,
         )
 
-    def gz(c, d, blk):
-        return remote(tok.at[:, chunk(c)], xg.at[c, blk], gz_send.at[c, d - 1], gz_recv.at[c, d - 1], z_blk(d), core)
-
-    def gy(c, d):
-        src = tok.at[:, chunk(c)] if d == 0 else xg.at[c, z_blk(NZ - d)]
-        return remote(src, xg.at[c, z_blk(NZ - d)], gy_send.at[c, d], gy_recv.at[c, d], y_peer, core)
-
-    def gy_in(c, d):
-        blk = ((z + NZ - d) % NZ) * NY + (1 - y)
-        return remote(tok.at[:, chunk(c)], xg.at[c, blk], gy_send.at[c, d], gy_recv.at[c, d], y_peer, core)
-
-    for c in range(CHUNKS):
-        for d in range(1, NZ):
-            gz(c, d, me).start()
+    def gz(src, c, k_src, k_dst, blk_from, to):
+        return remote(src, xg.at[c, blk_from], gz_send.at[c, k_src], gz_recv.at[c, k_dst], to, core)
+
+    def own_in(c):
+        return gz(tok.at[:, chunk(c)], c, 0, 1 + inner, me, inward)
+
+    def own_out(c):
+        return gz(tok.at[:, chunk(c)], c, 1, 1, me, outward)
+
+    def on_in(c):
+        blk = place(1) * NY + y
+        return gz(xg.at[c, blk], c, 2, 3, blk, inward)
+
+    def on_out(c, k):
+        blk = place(k) * NY + y
+        return gz(xg.at[c, blk], c, k + 1, k, blk, outward)
+
+    def gz_in(c, k):
+        return gz(tok.at[:, chunk(c)], c, 0, k, place(k) * NY + y, inward)
+
+    def gy(c, k):
+        blk = place(k) * NY + y
+        src = tok.at[:, chunk(c)] if k == 0 else xg.at[c, blk]
+        return remote(src, xg.at[c, blk], gy_send.at[c, k], gy_recv.at[c, k], y_peer, core)
+
+    def gy_in(c, k):
+        blk = place(k) * NY + (1 - y)
+        return remote(tok.at[:, chunk(c)], xg.at[c, blk], gy_send.at[c, k], gy_recv.at[c, k], y_peer, core)
+
+    for c in range(CHUNKS):
+        own_in(c).start()
         gy(c, 0).start()
+
+        @pl.when(inner == 1)
+        def _():
+            own_out(c).start()
 
     for c in range(CHUNKS):
         xg[c, me] = tok[:, c * span:(c + 1) * span]
@@ -195,10 +222,14 @@
     cos_k[...] = jnp.cos(angle_k)
     sin_k[...] = jnp.sin(angle_k)
 
-    def pass_on(c):
-        for d in range(1, NZ):
-            gz(c, d, z_blk(NZ - d)).wait_recv()
-            gy(c, d).start()
+    def pass_on(c, k):
+        gz_in(c, k).wait_recv()
+
+        @pl.when(inner == 1)
+        def _():
+            (on_in(c) if k == 1 else on_out(c, k)).start()
+
+        gy(c, k).start()
 
     def project(c):
         def body(k, _):
@@ -212,18 +243,17 @@
             acc_ss[...] += folded
             scaled = (x * gain[:, deep]).astype(bf16)
             acc_q[...] += jnp.dot(scaled, wq[deep, :], preferred_element_type=f32)
-            both = jnp.concatenate([wk[deep, :], wv[deep, :]], axis=1)
-            acc_kv[...] += jnp.dot(scaled, both, preferred_element_type=f32)
+            acc_kv[...] += lax.dot_general(wkv[:, deep], scaled, NT, preferred_element_type=f32)
             return 0
 
         lax.fori_loop(0, span // tile, body, 0)
 
-    pass_on(0)
-    for c in range(CHUNKS):
-        if c + 1 < CHUNKS:
-            pass_on(c + 1)
-        for d in range(NZ):
-            gy_in(c, d).wait_recv()
+    for k in range(1, NZ):
+        for c in range(CHUNKS):
+            pass_on(c, k)
+    for c in range(CHUNKS):
+        for k in range(NZ):
+            gy_in(c, k).wait_recv()
         if c == 0:
             wk_copy.wait()
             wv_copy.wait()
@@ -234,7 +264,7 @@
     cc = lax.broadcasted_iota(jnp.int32, (2 * kvw, 2 * kvw), 1)
     at = ((rr // per_head) % 2) * kvw + (rr % per_head) * KV_HEADS + rr // (2 * per_head)
     picks = jnp.where(cc == at, 1.0, 0.0).astype(bf16)
-    turned = lax.dot_general(picks, acc_kv[...].astype(bf16), NT, preferred_element_type=f32)
+    turned = jnp.dot(picks, acc_kv[...].astype(bf16), preferred_element_type=f32)
     kv_send[...] = turned.astype(bf16).reshape(KV_HEADS, 2 * per_head, total)
     group = HEADS // KV_HEADS
 
@@ -279,14 +309,18 @@
         probs = (raised / jnp.sum(raised, axis=1, keepdims=True)).astype(bf16)
         ctx[:, own] = lax.dot_general(probs, values, NT, preferred_element_type=f32).astype(bf16)
 
-    def ry(c):
-        return remote(part.at[c, 1 - y], y_part.at[c], ry_send.at[c], ry_recv.at[c], y_peer, core)
-
-    def rz(c, d):
-        return remote(
-            summed.at[c, (z + d) % NZ], z_part.at[c, d - 1],
-            rz_send.at[c, d - 1], rz_recv.at[c, d - 1], z_blk(d), core,
-        )
+    def ry(c, k):
+        at = place(k)
+        return remote(part.at[c, 1 - y, at], y_part.at[c, k], ry_send.at[c, k], ry_recv.at[c, k], y_peer, core)
+
+    def rz(c, k, slot, to):
+        return remote(summed.at[c, k], z_part.at[c, slot], rz_send.at[c, k], rz_recv.at[c, slot], to, core)
+
+    END = {3: 3, 2: 2, 1: 0}
+    MIDDLE = {3: 1, 2: 4, 1: 0}
+
+    def rz_in(c, slot):
+        return rz(c, 1, slot, inward)
 
     def multiply(c):
         wo_copies[c].wait()
@@ -301,45 +335,66 @@
             return 0
 
         lax.fori_loop(0, span // tile, body, 0)
-        ry(c).start()
-
-    def add_y(c):
-        ry(c).wait_recv()
-
-        def body(k, _):
-            here = pl.ds(pl.multiple_of(k * tile, tile), tile)
-            summed[c, :, :, here] = (
-                part[c, y, :, :, here].astype(f32) + y_part[c, :, :, here].astype(f32)
+        for k in reversed(range(NZ)):
+            ry(c, k).start()
+
+    def reduce(c):
+        for k in reversed(range(1, NZ)):
+            ry(c, k).wait_recv()
+
+            @pl.when(inner == 0)
+            def _():
+                summed[c, k] = (part[c, y, place(k)].astype(f32) + y_part[c, k].astype(f32)).astype(bf16)
+                rz(c, k, END[k], inward).start()
+
+            @pl.when(inner == 1)
+            def _():
+                rz_in(c, k).wait_recv()
+                summed[c, k] = (
+                    part[c, y, place(k)].astype(f32) + y_part[c, k].astype(f32) + z_part[c, k].astype(f32)
+                ).astype(bf16)
+                rz(c, k, MIDDLE[k], outward if k == 1 else inward).start()
+
+    def finish(c):
+        ry(c, 0).wait_recv()
+        rz_in(c, 0).wait_recv()
+        found = part[c, y, z].astype(f32) + y_part[c, 0].astype(f32) + z_part[c, 0].astype(f32)
+
+        @pl.when(inner == 0)
+        def _():
+            out[:, c * span:(c + 1) * span] = found.astype(bf16)
+
+        @pl.when(inner == 1)
+        def _():
+            rz_in(c, 4).wait_recv()
+            out[:, c * span:(c + 1) * span] = (
+                part[c, y, z].astype(f32) + y_part[c, 0].astype(f32)
+                + z_part[c, 0].astype(f32) + z_part[c, 4].astype(f32)
             ).astype(bf16)
-            return 0
-
-        lax.fori_loop(0, span // tile, body, 0)
-        for d in range(1, NZ):
-            rz(c, d).start()
-
-    def add_z(c):
-        for d in range(1, NZ):
-            rz(c, d).wait_recv()
-        found = summed[c, z].astype(f32)
-        for d in range(1, NZ):
-            found = found + z_part[c, d - 1].astype(f32)
-        out[:, c * span:(c + 1) * span] = found.astype(bf16)
 
     for c in range(CHUNKS):
         multiply(c)
         if c > 0:
-            add_y(c - 1)
-    add_y(CHUNKS - 1)
-    for c in range(CHUNKS):
-        add_z(c)
-
-    for c in range(CHUNKS):
-        for d in range(1, NZ):
-            gz(c, d, me).wait_send()
-            rz(c, d).wait_send()
-        for d in range(NZ):
-            gy(c, d).wait_send()
-        ry(c).wait_send()
+            reduce(c - 1)
+    reduce(CHUNKS - 1)
+    for c in range(CHUNKS):
+        finish(c)
+
+    for c in range(CHUNKS):
+        own_in(c).wait_send()
+
+        @pl.when(inner == 1)
+        def _():
+            own_out(c).wait_send()
+            on_in(c).wait_send()
+            for k in range(2, NZ):
+                on_out(c, k).wait_send()
+
+        for k in range(1, NZ):
+            rz(c, k, 0, inward).wait_send()
+        for k in range(NZ):
+            gy(c, k).wait_send()
+            ry(c, k).wait_send()
     for s, side in pairs:
         kv_copy(s, side, me, core).wait_send()
     ss_copy.wait_send()
@@ -365,12 +420,11 @@
         out_specs=vmem,
         scratch_shapes=[
             pltpu.VMEM((width, cols), bf16),
-            pltpu.VMEM((width, kvw), bf16),
-            pltpu.VMEM((width, kvw), bf16),
+            pltpu.VMEM((2 * kvw, width), bf16),
             pltpu.VMEM((cols, width), bf16),
             pltpu.VMEM((CHUNKS, n, rows, span), bf16),
             pltpu.VMEM((total, cols), f32),
-            pltpu.VMEM((total, 2 * kvw), f32),
+            pltpu.VMEM((2 * kvw, total), f32),
             pltpu.VMEM((total, HEAD), f32),
             pltpu.VMEM((total, cols), bf16),
             pltpu.VMEM((total, cols), bf16),
@@ -387,29 +441,29 @@
             pltpu.VMEM((CHUNKS, NY, NZ, rows, span), bf16),
             pltpu.VMEM((CHUNKS, NZ, rows, span), bf16),
             pltpu.VMEM((CHUNKS, NZ, rows, span), bf16),
-            pltpu.VMEM((CHUNKS, NZ - 1, rows, span), bf16),
+            pltpu.VMEM((CHUNKS, NZ + 1, rows, span), bf16),
             dma((CHUNKS,)),
             dma((CHUNKS,)),
             dma((2,)),
-            dma((CHUNKS, NZ - 1)),
-            dma((CHUNKS, NZ - 1)),
+            dma((CHUNKS, NZ + 1)),
+            dma((CHUNKS, NZ)),
             dma((CHUNKS, NZ)),
             dma((CHUNKS, NZ)),
             dma((2,)),
             dma((2,)),
             dma((n * WIDTH,)),
             dma((n * WIDTH,)),
-            dma((CHUNKS,)),
-            dma((CHUNKS,)),
-            dma((CHUNKS, NZ - 1)),
-            dma((CHUNKS, NZ - 1)),
+            dma((CHUNKS, NZ)),
+            dma((CHUNKS, NZ)),
+            dma((CHUNKS, NZ)),
+            dma((CHUNKS, NZ + 1)),
         ],
         compiler_params=pltpu.CompilerParams(
             collective_id=0, has_side_effects=True, vmem_limit_bytes=60 * 1024 * 1024
         ),
         name="attention_block",
     )(
-        tokens, norm_gain.reshape(1, width), w_query, w_key, w_value, w_output,
+        tokens, norm_gain.reshape(1, width), w_query, w_key.T, w_value.T, w_output,
         seq_ids.reshape(1, total),
     )
 

time: 86.3 us -> 75.2 us (0.87)
  Pallas kernels: 78.9 us -> 73.4 us
  local copies, waits for them, and re-layouts: 7.17 us -> 1.67 us
    unnamed x3 -> x1, local copies, waits for them, and re-layouts: 7.17 us -> 1.67 us
    pallas_call x1, Pallas kernels: 78.9 us -> 73.4 us  [kernel_form(): pl.pallas_call(fused_kernel, out_shape=jax.ShapeDtypeStruct((rows, width)...]
where the time goes in v2:
time: 75.2 us; the launch traced here: 75.1 us
  Pallas kernels  73.4 us (98%)
  local copies, waits for them, and re-layouts  1.67 us (2%)
    pallas_call x1, Pallas kernels, kernel_form(): pl.pallas_call(fused_kernel, out_shape=jax.ShapeDtypeStruct((rows, width)...  73.4 us
    unnamed x1, local copies, waits for them, and re-layouts  1.67 us

profile of v2, /device:TPU:0, one launch (start us, length us, event | category | flops | bytes accessed | tf_op | source)
XLA Modules:
  0.0 75.1 jit_solution(8824364227817520061)
XLA Ops:
  0.0 73.4 %attention_block.1 = bf16[16,8192]{1,0:T(8,128)(2,1)} custom-call(bf16[16,8192]{1,0:T(8,128)(2,1)} %tok.1, f32[1,8192]{1,0:T(1,128)} %bitcast.6, bf16[8192,1024]{1,0:T(8,128)(2,1)} %wq_hbm.1, bf16[64,8192]{1,0:T(8,128)(2,1)} %bitcast.4, bf16[64,8192]{1,0:T(8,128)(2,1)} %bitcast.5, bf16[1024,8192]{1,0:T(8,128)(2,1)} %wo_hbm.1, s32[1,128]{1,0:T(1,128)} %bitcast.7), custom_call_target="tpu_custom_call" | custom-call | tf_op jit(solution)/shard_map/attention_block/pallas_call | solution.py:416
  73.4 1.7 %copy.9 = bf16[16,8192]{1,0:T(8,128)(2,1)} copy(bf16[16,8192]{1,0:T(8,128)(2,1)} %attention_block.1) | data formatting | bytes 524288

commit v3 on v2

--- a/solution.py
+++ b/solution.py
@@ -335,11 +335,10 @@
             return 0
 
         lax.fori_loop(0, span // tile, body, 0)
-        for k in reversed(range(NZ)):
-            ry(c, k).start()
-
-    def reduce(c):
-        for k in reversed(range(1, NZ)):
+        ry(c, NZ - 1).start()
+
+    def reduce(c, k):
+        if True:
             ry(c, k).wait_recv()
 
             @pl.when(inner == 0)
@@ -374,9 +373,12 @@
 
     for c in range(CHUNKS):
         multiply(c)
-        if c > 0:
-            reduce(c - 1)
-    reduce(CHUNKS - 1)
+    for k in reversed(range(NZ - 1)):
+        for c in range(CHUNKS):
+            ry(c, k).start()
+    for k in reversed(range(1, NZ)):
+        for c in range(CHUNKS):
+            reduce(c, k)
     for c in range(CHUNKS):
         finish(c)
 

time: 75.2 us -> 67.1 us (0.89)
  Pallas kernels: 73.4 us -> 65.3 us
    pallas_call x1, Pallas kernels: 73.4 us -> 65.3 us  [kernel_form(): pl.pallas_call(fused_kernel, out_shape=jax.ShapeDtypeStruct((rows, width)...]
where the time goes in v3:
time: 67.1 us; the launch traced here: 67 us
  Pallas kernels  65.3 us (97%)
  local copies, waits for them, and re-layouts  1.67 us (2%)
    pallas_call x1, Pallas kernels, kernel_form(): pl.pallas_call(fused_kernel, out_shape=jax.ShapeDtypeStruct((rows, width)...  65.3 us
    unnamed x1, local copies, waits for them, and re-layouts  1.67 us

profile of v3, /device:TPU:0, one launch (start us, length us, event | category | flops | bytes accessed | tf_op | source)
XLA Modules:
  0.0 67.0 jit_solution(12024303486509490841)
XLA Ops:
  0.0 65.3 %attention_block.1 = bf16[16,8192]{1,0:T(8,128)(2,1)} custom-call(bf16[16,8192]{1,0:T(8,128)(2,1)} %tok.1, f32[1,8192]{1,0:T(1,128)} %bitcast.6, bf16[8192,1024]{1,0:T(8,128)(2,1)} %wq_hbm.1, bf16[64,8192]{1,0:T(8,128)(2,1)} %bitcast.4, bf16[64,8192]{1,0:T(8,128)(2,1)} %bitcast.5, bf16[1024,8192]{1,0:T(8,128)(2,1)} %wo_hbm.1, s32[1,128]{1,0:T(1,128)} %bitcast.7), custom_call_target="tpu_custom_call" | custom-call | tf_op jit(solution)/shard_map/attention_block/pallas_call | solution.py:418
  65.3 1.7 %copy.9 = bf16[16,8192]{1,0:T(8,128)(2,1)} copy(bf16[16,8192]{1,0:T(8,128)(2,1)} %attention_block.1) | data formatting | bytes 524288
